TPU v7x, 32 devices: a whole 2x2x4 slice. The times are simulated.
32 devices in a mesh: ctx: 16 (over z, y, x), tp: 2 (over core).
Axes of the slice: x: 2, y: 2, z: 4, core: 2. Of those that a mesh axis runs over, the one named last changes fastest.
Arguments:
- queries: bfloat16 [2, 2048, 4096], P(None, 'ctx', 'tp'), may hold values from -6 to 6
- key_input: bfloat16 [2, 2048, 4096], P(None, 'ctx', 'tp'), may hold values from -6 to 6
- value_input: bfloat16 [2, 2048, 4096], P(None, 'ctx', 'tp'), may hold values from -6 to 6
- filters: bfloat16 [128, 256], P(None, 'tp'), may hold values from -0.5 to 0.5
- skip_gain: float32 [4096], P('tp'), may hold values from -4 to 4
- grad_output: bfloat16 [2, 2048, 4096], P(None, 'ctx', 'tp'), may hold values from -120 to 120
Outputs:
- mixed: bfloat16 [2, 2048, 4096], P(None, 'ctx', 'tp')
- grad_queries: bfloat16 [2, 2048, 4096], P(None, 'ctx', 'tp')
- grad_keys: bfloat16 [2, 2048, 4096], P(None, 'ctx', 'tp')
- grad_values: bfloat16 [2, 2048, 4096], P(None, 'ctx', 'tp')
- filter_update: float32 [128, 256], P(None, 'tp')
- skip_update: float32 [4096], P('tp')
All inputs are finite; a program needn't handle non-finite values.
Results may differ from a plain program's by a relative error of at most 0.0051.
Values may be sent and summed in bfloat16 or wider, within the bound.
A program may use at most 64 MiB of HBM per device.

v0:
```python
import jax
import jax.numpy as jnp
from jax import lax
from jax.sharding import PartitionSpec as P


def shifted(shard, axis, by):
    devices = lax.axis_size(axis)
    pairs = [(i, i + by) for i in range(devices) if 0 <= i + by < devices]
    return lax.ppermute(shard, axis, pairs)


def on_device(queries, key_input, value_input, filters, skip_gain, grad_output):
    row_count = queries.shape[1]
    channel_count = queries.shape[2]
    tap_count = filters.shape[0]
    filter_count = filters.shape[1]
    group_width = channel_count // filter_count
    tap_weights = jnp.repeat(filters.astype(jnp.float32), group_width, axis=1)
    keys_f32 = key_input.astype(jnp.float32)
    values_f32 = value_input.astype(jnp.float32)
    product = (keys_f32 * values_f32).astype(jnp.bfloat16)
    earlier_keys, earlier_values = shifted(
        (key_input[:, row_count - tap_count + 1 :], value_input[:, row_count - tap_count + 1 :]),
        "ctx",
        1,
    )
    earlier = (earlier_keys.astype(jnp.float32) * earlier_values.astype(jnp.float32)).astype(
        jnp.bfloat16
    )
    extended = jnp.concatenate([earlier, product], 1).astype(jnp.float32)
    product_f32 = product.astype(jnp.float32)
    mixer_sum = skip_gain * product_f32
    for tap in range(tap_count):
        start = tap_count - 1 - tap
        mixer_sum = mixer_sum + tap_weights[tap] * extended[:, start : start + row_count]
    queries_f32 = queries.astype(jnp.float32)
    grad_f32 = grad_output.astype(jnp.float32)
    mixed = (queries_f32 * mixer_sum).astype(jnp.bfloat16)
    grad_queries = (grad_f32 * mixer_sum).astype(jnp.bfloat16)
    grad_mixer = (grad_f32 * queries_f32).astype(jnp.bfloat16)
    later_rim = shifted(grad_mixer[:, : tap_count - 1], "ctx", -1)
    grad_ext = jnp.concatenate([grad_mixer, later_rim], 1).astype(jnp.float32)
    mixer_grad_f32 = grad_mixer.astype(jnp.float32)
    grad_product = skip_gain * mixer_grad_f32
    tap_rows = []
    for tap in range(tap_count):
        grad_product = grad_product + tap_weights[tap] * grad_ext[:, tap : tap + row_count]
        start = tap_count - 1 - tap
        tap_rows.append(
            jnp.sum(mixer_grad_f32 * extended[:, start : start + row_count], axis=(0, 1))
        )
    grad_keys = (grad_product * values_f32).astype(jnp.bfloat16)
    grad_values = (grad_product * keys_f32).astype(jnp.bfloat16)
    channel_sums = jnp.stack(tap_rows, 0)
    owner = jnp.arange(channel_count, dtype=jnp.int32)[:, None] // group_width
    selector = (owner == jnp.arange(filter_count, dtype=jnp.int32)[None, :]).astype(jnp.float32)
    filter_local = jnp.dot(
        channel_sums, selector, precision=lax.Precision.HIGHEST, preferred_element_type=jnp.float32
    )
    skip_local = jnp.sum(mixer_grad_f32 * product_f32, axis=(0, 1))
    filter_entries = tap_count * filter_count * lax.axis_size("tp")
    skip_entries = skip_gain.shape[0] * lax.axis_size("tp")
    filter_grad, skip_grad = lax.psum((filter_local, skip_local), "ctx")
    filter_square, skip_square = lax.psum(
        (jnp.sum(filter_grad * filter_grad), jnp.sum(skip_grad * skip_grad)), "tp"
    )
    filter_update = filter_grad / jnp.sqrt(filter_square / filter_entries + 1e-06)
    skip_update = skip_grad / jnp.sqrt(skip_square / skip_entries + 1e-06)
    return (mixed, grad_queries, grad_keys, grad_values, filter_update, skip_update)


def solution(mesh):
    return jax.shard_map(
        on_device,
        mesh=mesh,
        in_specs=(
            P(None, "ctx", "tp"),
            P(None, "ctx", "tp"),
            P(None, "ctx", "tp"),
            P(None, "tp"),
            P("tp"),
            P(None, "ctx", "tp"),
        ),
        out_specs=(
            P(None, "ctx", "tp"),
            P(None, "ctx", "tp"),
            P(None, "ctx", "tp"),
            P(None, "ctx", "tp"),
            P(None, "tp"),
            P("tp"),
        ),
        check_vma=False,
    )
```

profile of v0, /device:TPU:0, one launch (start us, length us, event | category | flops | bytes accessed | tf_op | source)
XLA Modules:
  0.0 406.9 jit_solution(11436752719953300248)
XLA Ops:
  7.2 2.5 slice.1932
  9.8 4.9 %collective-permute-start.1 = (bf16[2,127,2048]{2,1,0:T(8,128)(2,1)}, bf16[2,127,2048]{2,1,0:T(8,128)(2,1)S(1)}, u32[]{:S(2)}, u32[]{:S(2)}) collective-permute-start(bf16[2,127,2048]{2,1,0:T(8,128)(2,1)} %slice.1932), channel_id=1, source_target_pairs={{0,2},{2,4},{4,6},{6,8},{8,10},{10,12},{12,14},{14,16},{16,18},{18... | collective-permute-start | bytes 3121160 | tf_op jit(solution)/shard_map/ppermute | solution.py:10
  14.7 1.2 slice.1931
  15.9 4.3 %collective-permute-start = (bf16[2,127,2048]{2,1,0:T(8,128)(2,1)}, bf16[2,127,2048]{2,1,0:T(8,128)(2,1)}, u32[]{:S(2)}, u32[]{:S(2)}) collective-permute-start(bf16[2,127,2048]{2,1,0:T(8,128)(2,1)} %slice.1931), channel_id=1, source_target_pairs={{0,2},{2,4},{4,6},{6,8},{8,10},{10,12},{12,14},{14,16},{16,18},{18... | collective-permute-start | bytes 3121160 | tf_op jit(solution)/shard_map/ppermute | solution.py:10
  72.2 0.7 broadcast_in_dim.587
  73.6 0.7 broadcast_in_dim.585
  80.6 0.7 broadcast_in_dim.575
  83.4 0.7 broadcast_in_dim.571
  86.2 0.7 broadcast_in_dim.567
  90.4 0.7 broadcast_in_dim.561
  105.6 0.7 broadcast_in_dim.539
  109.9 0.7 broadcast_in_dim.533
  113.7 1.6 multiply_convert_fusion
  116.9 55.7 %fusion.29 = (bf16[2,128,2048]{2,1,0:T(8,128)(2,1)}, f32[2,128,2048]{2,1,0:T(8,128)S(1)}) fusion(bf16[2,128,2048]{2,1,0:T(8,128)(2,1)S(1)} %copy-done.4, f32[2,255,2048]{2,1,0:T(8,128)S(1)} %maximum_convert_fusion, f32[2048]{0:T(1024)S(1)} %broadcast_in_dim.772, f32[2048]{0:T(1024)S(1)} %broadcast_in_dim.770, f32[2048]{0:T(1024)S(1)} %broadcast_in_dim.768, ...), kind=kLoop, calls=%fused_computation.166 | loop fusion | flops 136839168 | bytes 274735104 | tf_op jit(solution)/shard_map/convert_element_type | solution.py:40
  172.6 2.6 fusion.176
  175.2 5.7 %fusion.178 = (f32[2048]{0:T(1024)}, f32[2048]{0:T(1024)}, f32[2048]{0:T(1024)}, f32[2048]{0:T(1024)}, f32[2048]{0:T(1024)}, /*index=5*/f32[2048]{0:T(1024)}, f3...) fusion(bf16[2,128,2048]{2,1,0:T(8,128)(2,1)S(1)} %get-tuple-ele, ...), kind=kLoop, calls=%fused_computation.315 | loop fusion | flops 19361792 | bytes 38944768 | tf_op jit(solution)/shard_map/reduce_sum | solution.py:51
  180.8 5.7 %fusion.179 = (f32[2048]{0:T(1024)}, f32[2048]{0:T(1024)}, f32[2048]{0:T(1024)}, f32[2048]{0:T(1024)}, f32[2048]{0:T(1024)}, /*index=5*/f32[2048]{0:T(1024)}, f3...) fusion(bf16[2,128,2048]{2,1,0:T(8,128)(2,1)S(1)} %get-tuple-ele, ...), kind=kLoop, calls=%fused_computation.316 | loop fusion | flops 19361792 | bytes 38944768 | tf_op jit(solution)/shard_map/reduce_sum | solution.py:51
  186.5 5.7 %fusion.180 = (f32[2048]{0:T(1024)}, f32[2048]{0:T(1024)}, f32[2048]{0:T(1024)}, f32[2048]{0:T(1024)}, f32[2048]{0:T(1024)}, /*index=5*/f32[2048]{0:T(1024)}, f3...) fusion(bf16[2,128,2048]{2,1,0:T(8,128)(2,1)S(1)} %get-tuple-ele, ...), kind=kLoop, calls=%fused_computation.317 | loop fusion | flops 19361792 | bytes 38944768 | tf_op jit(solution)/shard_map/reduce_sum | solution.py:51
  192.2 5.7 %fusion.181 = (f32[2048]{0:T(1024)}, f32[2048]{0:T(1024)}, f32[2048]{0:T(1024)}, f32[2048]{0:T(1024)}, f32[2048]{0:T(1024)}, /*index=5*/f32[2048]{0:T(1024)}, f3...) fusion(bf16[2,128,2048]{2,1,0:T(8,128)(2,1)S(1)} %get-tuple-ele, ...), kind=kLoop, calls=%fused_computation.318 | loop fusion | flops 19361792 | bytes 38944768 | tf_op jit(solution)/shard_map/reduce_sum | solution.py:51
  197.9 5.7 %fusion.182 = (f32[2048]{0:T(1024)}, f32[2048]{0:T(1024)}, f32[2048]{0:T(1024)}, f32[2048]{0:T(1024)}, f32[2048]{0:T(1024)}, /*index=5*/f32[2048]{0:T(1024)}, f3...) fusion(bf16[2,128,2048]{2,1,0:T(8,128)(2,1)S(1)} %get-tuple-ele, ...), kind=kLoop, calls=%fused_computation.319 | loop fusion | flops 19361792 | bytes 38944768 | tf_op jit(solution)/shard_map/reduce_sum | solution.py:51
  203.5 5.7 %fusion.183 = (f32[2048]{0:T(1024)}, f32[2048]{0:T(1024)}, f32[2048]{0:T(1024)}, f32[2048]{0:T(1024)}, f32[2048]{0:T(1024)}, /*index=5*/f32[2048]{0:T(1024)}, f3...) fusion(bf16[2,128,2048]{2,1,0:T(8,128)(2,1)S(1)} %get-tuple-ele, ...), kind=kLoop, calls=%fused_computation.320 | loop fusion | flops 19361792 | bytes 38944768 | tf_op jit(solution)/shard_map/reduce_sum | solution.py:51
  209.3 1.3 collective-permute-start.2
  210.5 5.7 %fusion.177 = (f32[2048]{0:T(1024)}, f32[2048]{0:T(1024)}, f32[2048]{0:T(1024)}, f32[2048]{0:T(1024)}, f32[2048]{0:T(1024)}, /*index=5*/f32[2048]{0:T(1024)}, f3...) fusion(bf16[2,128,2048]{2,1,0:T(8,128)(2,1)S(1)} %get-tuple-ele, ...), kind=kLoop, calls=%fused_computation.314 | loop fusion | flops 19361792 | bytes 38944768 | tf_op jit(solution)/shard_map/reduce_sum | solution.py:51
  216.2 14.6 %stack.515 = f32[128,2048]{1,0:T(8,128)S(1)} concatenate(f32[1,2048]{1,0:T(1,128)} %bitcast.484, f32[1,2048]{1,0:T(1,128)} %bitcast.483, f32[1,2048]{1,0:T(1,128)} %bitcast.482, f32[1,2048]{1,0:T(1,128)} %bitcast.481, f32[1,2048]{1,0:T(1,128)} %bitcast.480, f32[1,2048]{1,0:T(1,128)} %bitcast.485, f32[1,2048]{1,0:T(1,128)} %bitcast.486, f32[1,2048]{1,0:T(1,128)} %bitcast.487, ...), dimensions={0} | concatenate | bytes 2097152 | tf_op jit(solution)/shard_map/stack | solution.py:55
  230.9 2.2 fusion.288
  233.1 41.5 %psum.30 = f32[2048]{0:T(1024)S(1)} all-reduce(f32[2048]{0:T(1024)} %get-tuple-element.134), channel_id=1, replica_groups=mesh['ctx'=16,'tp'=2] {'ctx'}, use_global_device_ids=true, to_apply=%region_132.133 | all-reduce | flops 2048 | bytes 16384 | tf_op jit(solution)/shard_map/psum | solution.py:64
  275.1 61.4 %all-reduce.3.cloned.1.call-done = f32[128,128]{1,0:T(8,128)} async-done(((f32[128,128]{1,0:T(8,128)}), f32[128,128]{1,0:T(8,128)}) %all-reduce.3.cloned.1.call-update) | async-done | bytes 65552 | tf_op jit(solution)/shard_map/psum | solution.py:64
  336.6 1.5 multiply_reduce_fusion
  338.0 3.1 all-reduce
  343.1 1.5 broadcast_divide_fusion
  346.2 52.6 %fusion.1 = (bf16[2,128,2048]{2,1,0:T(8,128)(2,1)}, f32[2,128,2048]{2,1,0:T(8,128)S(1)}) fusion(bf16[2,128,2048]{2,1,0:T(8,128)(2,1)S(1)} %copy-done.1, f32[2,255,2048]{2,1,0:T(8,128)S(1)} %maximum_convert_fusion.1, f32[2048]{0:T(1024)S(1)} %broadcast_in_dim.772, f32[2048]{0:T(1024)S(1)} %broadcast_in_dim.770, f32[2048]{0:T(1024)S(1)} %broadcast_in_dim.768, ...), kind=kLoop, calls=%fused_computation.138 | loop fusion | flops 136839168 | bytes 274735104 | tf_op jit(solution)/shard_map/convert_element_type | solution.py:54
  398.8 1.3 fusion.3
  (433 shorter events, 90.6 us)
Async XLA Ops:
  7.2 7.5 %copy-start = (bf16[2,128,2048]{2,1,0:T(8,128)(2,1)S(1)}, bf16[2,128,2048]{2,1,0:T(8,128)(2,1)}, u32[]{:S(2)}) copy-start(bf16[2,128,2048]{2,1,0:T(8,128)(2,1)} %param.7) | copy-start | bytes 3145732
  7.2 13.0 %copy-start.82 = (bf16[128,128]{1,0:T(8,128)(2,1)S(1)}, bf16[128,128]{1,0:T(8,128)(2,1)}, u32[]{:S(2)}) copy-start(bf16[128,128]{1,0:T(8,128)(2,1)} %param.9) | copy-start | bytes 98308
  7.2 329.4 %all-reduce.3.cloned.1.call-start = ((), (), s32[]{:S(2)}) async-start(), calls=%async_computation | async-start | bytes 131072 | tf_op jit(solution)/shard_map/psum | solution.py:64
  9.8 103.9 %collective-permute-start.1 = (bf16[2,127,2048]{2,1,0:T(8,128)(2,1)}, bf16[2,127,2048]{2,1,0:T(8,128)(2,1)S(1)}, u32[]{:S(2)}, u32[]{:S(2)}) collective-permute-start(bf16[2,127,2048]{2,1,0:T(8,128)(2,1)} %slice.1932), channel_id=1, source_target_pairs={{0,2},{2,4},{4,6},{6,8},{8,10},{10,12},{12,14},{14,16},{16,18},{18... | collective-permute-start | bytes 3121160 | tf_op jit(solution)/shard_map/ppermute | solution.py:10
  15.9 97.8 %collective-permute-start = (bf16[2,127,2048]{2,1,0:T(8,128)(2,1)}, bf16[2,127,2048]{2,1,0:T(8,128)(2,1)}, u32[]{:S(2)}, u32[]{:S(2)}) collective-permute-start(bf16[2,127,2048]{2,1,0:T(8,128)(2,1)} %slice.1931), channel_id=1, source_target_pairs={{0,2},{2,4},{4,6},{6,8},{8,10},{10,12},{12,14},{14,16},{16,18},{18... | collective-permute-start | bytes 3121160 | tf_op jit(solution)/shard_map/ppermute | solution.py:10
  71.5 41.8 %copy-start.2 = (bf16[2,128,2048]{2,1,0:T(8,128)(2,1)S(1)}, bf16[2,128,2048]{2,1,0:T(8,128)(2,1)}, u32[]{:S(2)}) copy-start(bf16[2,128,2048]{2,1,0:T(8,128)(2,1)} %param.8) | copy-start | bytes 3145732
  115.3 1.2 copy-start.4
  116.9 55.7 %copy-start.5 = (bf16[2,128,2048]{2,1,0:T(8,128)(2,1)S(1)}, bf16[2,128,2048]{2,1,0:T(8,128)(2,1)}, u32[]{:S(2)}) copy-start(bf16[2,128,2048]{2,1,0:T(8,128)(2,1)} %param.6) | copy-start | bytes 3145732
  209.3 135.7 %collective-permute-start.2 = (bf16[2,127,2048]{2,1,0:T(8,128)(2,1)S(1)}, bf16[2,127,2048]{2,1,0:T(8,128)(2,1)S(1)}, u32[]{:S(2)}, u32[]{:S(2)}) collective-permute-start(bf16[2,127,2048]{2,1,0:T(8,128)(2,1)S(1)} %bitcast.386), channel_id=1, source_target_pairs={{2,0},{4,2},{6,4},{8,6},{10,8},{12,10},{14,12},{16,14},{18,16},{20... | collective-permute-start | bytes 3121160 | tf_op jit(solution)/shard_map/ppermute | solution.py:10
  344.6 1.2 copy-start.1
  344.6 1.2 copy-start.15
  344.6 1.2 copy-start.17
  344.6 1.2 copy-start.19
  344.6 1.2 copy-start.21
  344.6 1.2 copy-start.23
  344.6 1.2 copy-start.25
  344.6 1.2 copy-start.27
  344.6 1.2 copy-start.29
  344.7 1.2 copy-start.31
  344.7 1.2 copy-start.33
  344.7 1.2 copy-start.35
  344.7 1.2 copy-start.37
  344.7 1.2 copy-start.39
  344.7 1.2 copy-start.41
  344.7 1.2 copy-start.43
  344.7 1.2 copy-start.45
  344.7 1.2 copy-start.47
  344.8 1.2 copy-start.49
  344.8 1.2 copy-start.51
  344.8 1.2 copy-start.53
  344.8 1.2 copy-start.55
  346.2 52.6 %copy-start.3 = (bf16[2,128,2048]{2,1,0:T(8,128)(2,1)S(1)}, bf16[2,128,2048]{2,1,0:T(8,128)(2,1)}, u32[]{:S(2)}) copy-start(bf16[2,128,2048]{2,1,0:T(8,128)(2,1)} %param.8) | copy-start | bytes 3145732
  (55 other events, 65.8 us)
Sparse Core Ops, SparseCore 0:
  233.2 103.3 all-reduce.2
where the time goes:
time: 409 us; the launch traced here: 407 us
  other arithmetic  160 us (39%)
  local copies, waits for them, and re-layouts  112 us (27%)
  waiting for transfers between devices  61.5 us (15%)
  blocking collectives  44.6 us (11%)
  between operations  16.9 us (4%)
  starting transfers between devices  10.5 us (3%)
    broadcast_in_dim x256, local copies, waits for them, and re-layouts, on_device(): tap_weights = jnp.repeat(filters.astype(jnp.float32), group_width, axis=1)  90.9 us
    psum x1, waiting for transfers between devices, on_device(): filter_grad, skip_grad = lax.psum((filter_local, skip_local), 'ctx')  61.4 us
    convert_element_type x1, other arithmetic, on_device(): grad_queries = (grad_f32 * mixer_sum).astype(jnp.bfloat16)  55.7 us
    convert_element_type x1, other arithmetic, on_device(): grad_values = (grad_product * keys_f32).astype(jnp.bfloat16)  52.6 us
    reduce_sum x8, other arithmetic, on_device(): jnp.sum(mixer_grad_f32 * extended[:, start:start + row_count], axis=(0, 1))  42.3 us
    psum x1, blocking collectives, on_device(): filter_grad, skip_grad = lax.psum((filter_local, skip_local), 'ctx')  41.5 us
    another operation x1, local copies, waits for them, and re-layouts, on_device(): channel_sums = jnp.stack(tap_rows, 0)  14.6 us
    ppermute x3, starting transfers between devices, shifted(): return lax.ppermute(shard, axis, pairs)  10.5 us
  transfers between devices with their start and end apart: 4, of which 1 were waited for; matrix products, arithmetic and copies ran while one was open for 30% of the time, Pallas kernels for 0%

commit v1 on v0

v1 whole, which is shorter than its diff:
```python
import functools

import jax
import jax.numpy as jnp
from jax import lax
from jax.experimental import pallas as pl
from jax.experimental.pallas import tpu as pltpu
from jax.sharding import PartitionSpec as P

MESH = pl.DeviceIdType.MESH
LANES = 128
FOLD = 16


def step_kernel(
    n,
    groups,
    in_flight,
    entries,
    filt_ref,
    skip_ref,
    q_ref,
    k_ref,
    v_ref,
    go_ref,
    mixed_ref,
    gq_ref,
    gk_ref,
    gv_ref,
    fu_ref,
    su_ref,
    prod,
    gmix,
    prod_halo,
    gmix_halo,
    fwd_rows,
    bwd_rows,
    fwd_band,
    bwd_band,
    part,
    terms,
    reduced,
    squares,
    p_send,
    p_recv,
    g_send,
    g_recv,
    rs_send,
    rs_recv,
    ag_send,
    ag_recv,
    sq_send,
    sq_recv,
):
    me = lax.axis_index("ctx")
    core = lax.axis_index("tp")
    batch, rows = q_ref.shape[0], q_ref.shape[1]
    taps = filt_ref.shape[0]
    per_group = fwd_band.shape[0] // rows
    width = LANES // per_group
    fil_entries, skip_entries = entries

    barrier = pltpu.get_barrier_semaphore()

    @pl.loop(1, n)
    def _(i):
        pl.semaphore_signal(
            barrier, inc=1, device_id=(lax.rem(me + i, n), core), device_id_type=MESH
        )

    pl.semaphore_signal(barrier, inc=1, device_id=(me, 1 - core), device_id_type=MESH)

    def p_copy(g):
        return pltpu.make_async_remote_copy(
            src_ref=prod.at[g],
            dst_ref=prod_halo.at[g],
            send_sem=p_send.at[g],
            recv_sem=p_recv.at[g],
            device_id=(lax.rem(me + 1, n), core),
            device_id_type=MESH,
        )

    def g_copy(g):
        return pltpu.make_async_remote_copy(
            src_ref=gmix.at[g],
            dst_ref=gmix_halo.at[g],
            send_sem=g_send.at[g],
            recv_sem=g_recv.at[g],
            device_id=(lax.rem(me + n - 1, n), core),
            device_id_type=MESH,
        )

    def start_halo(g):
        @pl.when(me < n - 1)
        def _():
            p_copy(g).start()

        @pl.when(me > 0)
        def _():
            g_copy(g).start()

    def lanes_of(g):
        return pl.ds(pl.multiple_of(g * LANES, LANES), LANES)

    def factors(g):
        cols = lanes_of(g)
        for b in range(batch):
            kf = k_ref[b, :, cols].astype(jnp.float32)
            vf = v_ref[b, :, cols].astype(jnp.float32)
            prod[g, b] = (kf * vf).astype(jnp.bfloat16)
            qf = q_ref[b, :, cols].astype(jnp.float32)
            of = go_ref[b, :, cols].astype(jnp.float32)
            gmix[g, b] = (qf * of).astype(jnp.bfloat16)

    factors(0)
    pl.semaphore_wait(barrier, n)
    start_halo(0)

    @pl.loop(1, groups)
    def _(g):
        factors(g)

        @pl.when(g < in_flight)
        def _():
            start_halo(g)

    @pl.when(me == 0)
    def _():
        prod_halo[...] = jnp.zeros_like(prod_halo)

    @pl.when(me == n - 1)
    def _():
        gmix_halo[...] = jnp.zeros_like(gmix_halo)

    filt_t = filt_ref[...].astype(jnp.float32).T
    src = lax.broadcasted_iota(jnp.int32, (taps, taps), 0)
    dst = lax.broadcasted_iota(jnp.int32, (taps, taps), 1)
    mirror = (lax.rem(src + dst, taps) == 0).astype(jnp.bfloat16)
    bwd_rows[...] = filt_t
    fwd_rows[...] = jnp.dot(
        filt_t.astype(jnp.bfloat16), mirror, preferred_element_type=jnp.float32
    )

    t_idx = lax.broadcasted_iota(jnp.int32, (rows, taps), 0)
    s_idx = lax.broadcasted_iota(jnp.int32, (rows, taps), 1)

    def build_bands(g):
        first = pl.ds(pl.multiple_of(g * per_group, per_group), per_group)
        fwd_taps = fwd_rows[first, :]
        bwd_taps = bwd_rows[first, :]
        for f in range(per_group):
            at = slice(f * rows, (f + 1) * rows)
            turned = pltpu.roll(
                jnp.broadcast_to(fwd_taps[f : f + 1], (rows, taps)), 0, 1, stride=1, stride_axis=0
            )
            fwd_band[at, :taps] = jnp.where(s_idx > t_idx, turned, 0.0).astype(jnp.bfloat16)
            fwd_band[at, taps:] = jnp.where(s_idx <= t_idx, turned, 0.0).astype(jnp.bfloat16)
            turned = pltpu.roll(
                jnp.broadcast_to(bwd_taps[f : f + 1], (rows, taps)), 0, 1, stride=1, stride_axis=0
            )
            bwd_band[at, :taps] = jnp.where(s_idx >= t_idx, turned, 0.0).astype(jnp.bfloat16)
            bwd_band[at, taps:] = jnp.where(s_idx < t_idx, turned, 0.0).astype(jnp.bfloat16)

    lane_filter = lax.rem(
        lax.broadcasted_iota(jnp.int32, (rows, batch * LANES), 1), LANES
    ) // width
    row_filter = lax.broadcasted_iota(jnp.int32, (rows, batch * LANES), 0) // FOLD
    own_filter = (lane_filter == row_filter).astype(jnp.float32).astype(jnp.bfloat16)

    def banded(band, ext):
        every = jnp.dot(band[...], ext, preferred_element_type=jnp.float32)
        picked = every[:rows]
        for f in range(1, per_group):
            picked = jnp.where(lane_filter == f, every[f * rows : (f + 1) * rows], picked)
        return picked

    @pl.loop(0, groups)
    def _(g):
        cols = lanes_of(g)
        build_bands(g)

        @pl.when(me > 0)
        def _():
            p_copy(g).wait_recv()

        @pl.when(me < n - 1)
        def _():
            g_copy(g).wait_recv()

        @pl.when(g + in_flight < groups)
        def _():
            start_halo(g + in_flight)

        gain = skip_ref[pl.ds(g, 1), :]
        own_p = [prod[g, b] for b in range(batch)]
        own_g = [gmix[g, b] for b in range(batch)]
        ext_p = jnp.concatenate(
            [jnp.concatenate([prod_halo[g, b] for b in range(batch)], 1), jnp.concatenate(own_p, 1)], 0
        )
        ext_g = jnp.concatenate(
            [jnp.concatenate(own_g, 1), jnp.concatenate([gmix_halo[g, b] for b in range(batch)], 1)], 0
        )
        forward = banded(fwd_band, ext_p)
        backward = banded(bwd_band, ext_g)
        skip_sum = jnp.zeros((1, LANES), jnp.float32)
        for b in range(batch):
            pf = own_p[b].astype(jnp.float32)
            gf = own_g[b].astype(jnp.float32)
            at = slice(b * LANES, (b + 1) * LANES)
            mixer = forward[:, at] + gain * pf
            grad_p = backward[:, at] + gain * gf
            mixed_ref[b, :, cols] = (q_ref[b, :, cols].astype(jnp.float32) * mixer).astype(jnp.bfloat16)
            gq_ref[b, :, cols] = (go_ref[b, :, cols].astype(jnp.float32) * mixer).astype(jnp.bfloat16)
            gk_ref[b, :, cols] = (v_ref[b, :, cols].astype(jnp.float32) * grad_p).astype(jnp.bfloat16)
            gv_ref[b, :, cols] = (k_ref[b, :, cols].astype(jnp.float32) * grad_p).astype(jnp.bfloat16)
            skip_sum = skip_sum + jnp.sum(pf * gf, axis=0, keepdims=True)

        wide_p = jnp.concatenate(own_p, 1)
        lhs, rhs = [], []
        blank = jnp.zeros((2 * taps - taps - FOLD, batch * LANES), jnp.bfloat16)
        for a in range(rows // FOLD):
            piece = wide_p[a * FOLD : (a + 1) * FOLD]
            lhs.append(jnp.concatenate([piece] * per_group, 0) * own_filter)
            rhs.append(jnp.concatenate([ext_g[a * FOLD : a * FOLD + taps + FOLD], blank], 0))
        outer = lax.dot_general(
            jnp.concatenate(lhs, 1),
            jnp.concatenate(rhs, 1),
            (((1,), (1,)), ((), ())),
            preferred_element_type=jnp.float32,
        )
        span = outer.shape[1]
        halves = outer.reshape(per_group, 2, FOLD // 2, span)
        upper = halves[:, 0].reshape(per_group * FOLD // 2, span)
        lower = halves[:, 1].reshape(per_group * FOLD // 2, span)
        summed = upper + pltpu.roll(lower, span - FOLD // 2, 1)
        row_of = lax.rem(
            lax.broadcasted_iota(jnp.int32, summed.shape, 0), FOLD // 2
        )
        for bit in (4, 2, 1):
            summed = jnp.where(
                lax.rem(row_of // bit, 2) == 1, pltpu.roll(summed, span - bit, 1), summed
            )
        tap_sums = jnp.sum(summed.reshape(per_group, FOLD // 2, span), axis=1)
        part[g, :per_group, :] = tap_sums[:, :taps]
        part[g, per_group:, :] = jnp.broadcast_to(skip_sum, (part.shape[1] - per_group, LANES))

        @pl.when(me == g)
        def _():
            terms[n - 1] = part[g]

        @pl.when(me != g)
        def _():
            pltpu.make_async_remote_copy(
                src_ref=part.at[g],
                dst_ref=terms.at[lax.rem(me - g - 1 + n, n)],
                send_sem=rs_send,
                recv_sem=rs_recv,
                device_id=(g, core),
                device_id_type=MESH,
            ).start()

    def wait_bytes(buffer, count, sem):
        pltpu.make_async_copy(buffer.at[pl.ds(0, count)], buffer.at[pl.ds(0, count)], sem).wait()

    @pl.when(me < groups)
    def _():
        wait_bytes(terms, n - 1, rs_recv)
        total = terms[0]
        for i in range(1, n):
            total = total + terms[i]
        reduced[me] = total

        @pl.loop(1, n)
        def _(i):
            pltpu.make_async_remote_copy(
                src_ref=reduced.at[me],
                dst_ref=reduced.at[me],
                send_sem=ag_send,
                recv_sem=ag_recv,
                device_id=(lax.rem(me + i, n), core),
                device_id_type=MESH,
            ).start()

        wait_bytes(reduced, groups - 1, ag_recv)

    @pl.when(me >= groups)
    def _():
        wait_bytes(reduced, groups, ag_recv)

    fil = reduced[:, :per_group, :].reshape(groups * per_group, taps)
    skp = reduced[:, per_group, :]
    squares[0, 0:8, :] = jnp.sum((fil * fil).reshape(groups, per_group, taps), axis=0)
    squares[0, 8:16, :] = jnp.sum((skp * skp).reshape(groups // 8, 8, LANES), axis=0)
    swap = pltpu.make_async_remote_copy(
        src_ref=squares.at[0],
        dst_ref=squares.at[1],
        send_sem=sq_send,
        recv_sem=sq_recv,
        device_id=(me, 1 - core),
        device_id_type=MESH,
    )
    swap.start()
    fil_t = fil.T
    swap.wait()
    both = squares[0] + squares[1]
    fil_mean = jnp.sum(both[0:8]) / fil_entries
    skip_mean = jnp.sum(both[8:16]) / skip_entries
    fu_ref[...] = fil_t / jnp.sqrt(jnp.full(fil_t.shape, fil_mean, jnp.float32) + 1e-06)
    su_ref[...] = skp / jnp.sqrt(jnp.full(skp.shape, skip_mean, jnp.float32) + 1e-06)

    @pl.loop(0, groups)
    def _(g):
        @pl.when(me < n - 1)
        def _():
            p_copy(g).wait_send()

        @pl.when(me > 0)
        def _():
            g_copy(g).wait_send()

    @pl.when(me < groups)
    def _():
        wait_bytes(part, groups - 1, rs_send)
        wait_bytes(terms, n - 1, ag_send)

    @pl.when(me >= groups)
    def _():
        wait_bytes(part, groups, rs_send)


def on_device(in_flight, queries, key_input, value_input, filters, skip_gain, grad_output):
    batch, rows, channels = queries.shape
    taps, filter_count = filters.shape
    groups = channels // LANES
    per_group = filter_count // groups
    n = lax.axis_size("ctx")
    cores = lax.axis_size("tp")
    entries = (float(taps * filter_count * cores), float(channels * cores))
    vmem = pl.BlockSpec(memory_space=pltpu.VMEM)
    chunk = (groups, batch, rows, LANES)
    act = jax.ShapeDtypeStruct(queries.shape, jnp.bfloat16)
    outs = pl.pallas_call(
        functools.partial(step_kernel, n, groups, in_flight, entries),
        out_shape=(
            act,
            act,
            act,
            act,
            jax.ShapeDtypeStruct((taps, filter_count), jnp.float32),
            jax.ShapeDtypeStruct((groups, LANES), jnp.float32),
        ),
        in_specs=[vmem] * 6,
        out_specs=(vmem,) * 6,
        scratch_shapes=[
            pltpu.VMEM(chunk, jnp.bfloat16),
            pltpu.VMEM(chunk, jnp.bfloat16),
            pltpu.VMEM(chunk, jnp.bfloat16),
            pltpu.VMEM(chunk, jnp.bfloat16),
            pltpu.VMEM((filter_count, taps), jnp.float32),
            pltpu.VMEM((filter_count, taps), jnp.float32),
            pltpu.VMEM((per_group * rows, 2 * taps), jnp.bfloat16),
            pltpu.VMEM((per_group * rows, 2 * taps), jnp.bfloat16),
            pltpu.VMEM((groups, 16, LANES), jnp.float32),
            pltpu.VMEM((n, 16, LANES), jnp.float32),
            pltpu.VMEM((groups, 16, LANES), jnp.float32),
            pltpu.VMEM((2, 16, LANES), jnp.float32),
            pltpu.SemaphoreType.DMA((groups,)),
            pltpu.SemaphoreType.DMA((groups,)),
            pltpu.SemaphoreType.DMA((groups,)),
            pltpu.SemaphoreType.DMA((groups,)),
            pltpu.SemaphoreType.DMA,
            pltpu.SemaphoreType.DMA,
            pltpu.SemaphoreType.DMA,
            pltpu.SemaphoreType.DMA,
            pltpu.SemaphoreType.DMA,
            pltpu.SemaphoreType.DMA,
        ],
        compiler_params=pltpu.CompilerParams(
            collective_id=0, has_side_effects=True, vmem_limit_bytes=48 * 1024 * 1024
        ),
    )(filters, skip_gain.reshape(groups, LANES), queries, key_input, value_input, grad_output)
    return (*outs[:5], outs[5].reshape(channels))


def solution(mesh):
    act = P(None, "ctx", "tp")
    return jax.shard_map(
        functools.partial(on_device, 16),
        mesh=mesh,
        in_specs=(act, act, act, P(None, "tp"), P("tp"), act),
        out_specs=(act, act, act, act, P(None, "tp"), P("tp")),
        check_vma=False,
    )
```

time: 409 us -> 76.3 us (0.19)
  other arithmetic: 160 us -> 0 us
  local copies, waits for them, and re-layouts: 112 us -> 7.78 us
  Pallas kernels: 0 us -> 67.6 us
  waiting for transfers between devices: 61.5 us -> 0 us
  blocking collectives: 44.6 us -> 0 us
  between operations: 16.9 us -> 0.65 us
  starting transfers between devices: 10.5 us -> 0 us
    convert_element_type x8 -> x0, other arithmetic: 113 us -> none  [the longest x1 55.7 us: on_device(): grad_queries = (grad_f32 * mixer_sum).astype(jnp.bfloat16)]
    broadcast_in_dim x256 -> x0, local copies, waits for them, and re-layouts: 90.9 us -> none  [on_device(): tap_weights = jnp.repeat(filters.astype(jnp.float32), group_width, axis=1)]
    pallas_call x0 -> x1, Pallas kernels: none -> 67.6 us  [on_device(): pl.pallas_call(functools.partial(step_kernel, n, groups, in_flight, entri...]
    psum x1 -> x0, waiting for transfers between devices: 61.4 us -> none  [on_device(): filter_grad, skip_grad = lax.psum((filter_local, skip_local), 'ctx')]
    psum x2 -> x0, blocking collectives: 44.6 us -> none  [the longest x1 41.5 us: on_device(): filter_grad, skip_grad = lax.psum((filter_local, skip_local), 'ctx')]
    reduce_sum x10 -> x0, other arithmetic: 44.4 us -> none  [the longest x8 42.3 us: on_device(): jnp.sum(mixer_grad_f32 * extended[:, start:start + row_count], axis=(0, 1))]
    another operation x1 -> x0, local copies, waits for them, and re-layouts: 14.6 us -> none  [on_device(): channel_sums = jnp.stack(tap_rows, 0)]
    ppermute x3 -> x0, starting transfers between devices: 10.5 us -> none  [shifted(): return lax.ppermute(shard, axis, pairs)]
  transfers between devices with their start and end apart: 4 -> 0, of which waited for: 1 -> 0; matrix products, arithmetic and copies ran while one was open for 30% -> 0% of each run, Pallas kernels for 0% -> 0%
where the time goes in v1:
time: 76.3 us; the launch traced here: 76.1 us
  Pallas kernels  67.6 us (89%)
  local copies, waits for them, and re-layouts  7.78 us (10%)
    pallas_call x1, Pallas kernels, on_device(): pl.pallas_call(functools.partial(step_kernel, n, groups, in_flight, entri...  67.6 us
    unnamed x12, local copies, waits for them, and re-layouts  7.78 us

profile of v1, /device:TPU:0, one launch (start us, length us, event | category | flops | bytes accessed | tf_op | source)
XLA Modules:
  0.0 76.1 jit_solution(9104272603135435674)
XLA Ops:
  0.6 0.0 copy-start
  0.6 1.2 %copy-done = bf16[2,128,2048]{2,1,0:T(8,128)(2,1)S(1)} copy-done((bf16[2,128,2048]{2,1,0:T(8,128)(2,1)S(1)}, bf16[2,128,2048]{2,1,0:T(8,128)(2,1)}, u32[]{:S(2)}) %copy-start) | copy-done | bytes 1048600
  1.9 0.0 copy-start.1
  1.9 0.8 copy-done.1
  2.6 0.0 copy-start.2
  2.6 0.7 copy-done.2
  3.3 67.6 %shard_map.109 = (bf16[2,128,2048]{2,1,0:T(8,128)(2,1)S(1)}, bf16[2,128,2048]{2,1,0:T(8,128)(2,1)S(1)}, bf16[2,128,2048]{2,1,0:T(8,128)(2,1)S(1)}, bf16[2,128,20...) custom-call(bf16[128,128]{1,0:T(8,128)(2,1)S(1)} %copy-done.1, f32[16,128]{1,0:T(8,128)S(1)} %bitcast.2, ...), custom_call_target="tpu_custom_call" | custom-call | tf_op jit(solution)/shard_map/pallas_call | solution.py:342
  71.0 1.0 %copy.18 = bf16[2,128,2048]{2,1,0:T(8,128)(2,1)} copy(bf16[2,128,2048]{2,1,0:T(8,128)(2,1)S(1)} %get-tuple-element.24) | data formatting | bytes 2097152
  71.9 1.0 %copy.19 = bf16[2,128,2048]{2,1,0:T(8,128)(2,1)} copy(bf16[2,128,2048]{2,1,0:T(8,128)(2,1)S(1)} %get-tuple-element.25) | data formatting | bytes 2097152
  72.9 1.0 %copy.20 = bf16[2,128,2048]{2,1,0:T(8,128)(2,1)} copy(bf16[2,128,2048]{2,1,0:T(8,128)(2,1)S(1)} %get-tuple-element.26) | data formatting | bytes 2097152
  73.9 1.0 %copy.21 = bf16[2,128,2048]{2,1,0:T(8,128)(2,1)} copy(bf16[2,128,2048]{2,1,0:T(8,128)(2,1)S(1)} %get-tuple-element.27) | data formatting | bytes 2097152
  74.8 0.6 copy.22
  75.5 0.6 copy.23
Async XLA Ops:
  0.6 1.2 %copy-start = (bf16[2,128,2048]{2,1,0:T(8,128)(2,1)S(1)}, bf16[2,128,2048]{2,1,0:T(8,128)(2,1)}, u32[]{:S(2)}) copy-start(bf16[2,128,2048]{2,1,0:T(8,128)(2,1)} %q_ref.1) | copy-start | bytes 3145732
  1.9 0.8 copy-start.1
  2.6 0.7 copy-start.2

commit v2 on v1

--- a/solution.py
+++ b/solution.py
@@ -10,25 +10,30 @@
 MESH = pl.DeviceIdType.MESH
 LANES = 128
 FOLD = 16
+LOADS = 4
+AHEAD = 4
 
 
 def step_kernel(
     n,
     groups,
-    in_flight,
     entries,
     filt_ref,
     skip_ref,
-    q_ref,
-    k_ref,
-    v_ref,
-    go_ref,
+    q_hbm,
+    k_hbm,
+    v_hbm,
+    go_hbm,
     mixed_ref,
     gq_ref,
     gk_ref,
     gv_ref,
     fu_ref,
     su_ref,
+    q_ref,
+    k_ref,
+    v_ref,
+    go_ref,
     prod,
     gmix,
     prod_halo,
@@ -41,6 +46,7 @@
     terms,
     reduced,
     squares,
+    in_sem,
     p_send,
     p_recv,
     g_send,
@@ -60,6 +66,19 @@
     width = LANES // per_group
     fil_entries, skip_entries = entries
 
+    wide = q_hbm.shape[2] // LOADS
+    sources = ((q_hbm, q_ref), (go_hbm, go_ref), (k_hbm, k_ref), (v_hbm, v_ref))
+
+    def load(array, part_of):
+        src, dst = sources[array]
+        at = pl.ds(part_of * wide, wide)
+        return pltpu.make_async_copy(src.at[:, :, at], dst.at[:, :, at], in_sem.at[array, part_of])
+
+    for first in (0, 2):
+        for c in range(LOADS):
+            load(first, c).start()
+            load(first + 1, c).start()
+
     barrier = pltpu.get_barrier_semaphore()
 
     @pl.loop(1, n)
@@ -90,39 +109,38 @@
             device_id_type=MESH,
         )
 
-    def start_halo(g):
-        @pl.when(me < n - 1)
-        def _():
-            p_copy(g).start()
-
-        @pl.when(me > 0)
-        def _():
-            g_copy(g).start()
-
     def lanes_of(g):
         return pl.ds(pl.multiple_of(g * LANES, LANES), LANES)
 
-    def factors(g):
+    def times(out, left, right, g):
         cols = lanes_of(g)
         for b in range(batch):
-            kf = k_ref[b, :, cols].astype(jnp.float32)
-            vf = v_ref[b, :, cols].astype(jnp.float32)
-            prod[g, b] = (kf * vf).astype(jnp.bfloat16)
-            qf = q_ref[b, :, cols].astype(jnp.float32)
-            of = go_ref[b, :, cols].astype(jnp.float32)
-            gmix[g, b] = (qf * of).astype(jnp.bfloat16)
-
-    factors(0)
-    pl.semaphore_wait(barrier, n)
-    start_halo(0)
-
-    @pl.loop(1, groups)
-    def _(g):
-        factors(g)
-
-        @pl.when(g < in_flight)
-        def _():
-            start_halo(g)
+            lf = left[b, :, cols].astype(jnp.float32)
+            rf = right[b, :, cols].astype(jnp.float32)
+            out[g, b] = (lf * rf).astype(jnp.bfloat16)
+
+    per_load = groups // LOADS
+    for c in range(LOADS):
+        load(0, c).wait()
+        load(1, c).wait()
+        if c == 0:
+            pl.semaphore_wait(barrier, n)
+
+        @pl.loop(c * per_load, (c + 1) * per_load)
+        def _(g):
+            times(gmix, q_ref, go_ref, g)
+
+            @pl.when(me > 0)
+            def _():
+                g_copy(g).start()
+
+    for c in range(LOADS):
+        load(2, c).wait()
+        load(3, c).wait()
+
+        @pl.loop(c * per_load, (c + 1) * per_load)
+        def _(g):
+            times(prod, k_ref, v_ref, g)
 
     @pl.when(me == 0)
     def _():
@@ -144,22 +162,15 @@
     t_idx = lax.broadcasted_iota(jnp.int32, (rows, taps), 0)
     s_idx = lax.broadcasted_iota(jnp.int32, (rows, taps), 1)
 
-    def build_bands(g):
-        first = pl.ds(pl.multiple_of(g * per_group, per_group), per_group)
-        fwd_taps = fwd_rows[first, :]
-        bwd_taps = bwd_rows[first, :]
+    def build_band(band, tap_rows, g, left, right):
+        own = tap_rows[pl.ds(pl.multiple_of(g * per_group, per_group), per_group), :]
         for f in range(per_group):
             at = slice(f * rows, (f + 1) * rows)
             turned = pltpu.roll(
-                jnp.broadcast_to(fwd_taps[f : f + 1], (rows, taps)), 0, 1, stride=1, stride_axis=0
+                jnp.broadcast_to(own[f : f + 1], (rows, taps)), 0, 1, stride=1, stride_axis=0
             )
-            fwd_band[at, :taps] = jnp.where(s_idx > t_idx, turned, 0.0).astype(jnp.bfloat16)
-            fwd_band[at, taps:] = jnp.where(s_idx <= t_idx, turned, 0.0).astype(jnp.bfloat16)
-            turned = pltpu.roll(
-                jnp.broadcast_to(bwd_taps[f : f + 1], (rows, taps)), 0, 1, stride=1, stride_axis=0
-            )
-            bwd_band[at, :taps] = jnp.where(s_idx >= t_idx, turned, 0.0).astype(jnp.bfloat16)
-            bwd_band[at, taps:] = jnp.where(s_idx < t_idx, turned, 0.0).astype(jnp.bfloat16)
+            band[at, :taps] = jnp.where(left, turned, 0.0).astype(jnp.bfloat16)
+            band[at, taps:] = jnp.where(right, turned, 0.0).astype(jnp.bfloat16)
 
     lane_filter = lax.rem(
         lax.broadcasted_iota(jnp.int32, (rows, batch * LANES), 1), LANES
@@ -174,43 +185,61 @@
             picked = jnp.where(lane_filter == f, every[f * rows : (f + 1) * rows], picked)
         return picked
 
+    def send_product(g):
+        @pl.when(me < n - 1)
+        def _():
+            p_copy(g).start()
+
+    def forward_step(g):
+        cols = lanes_of(g)
+        build_band(fwd_band, fwd_rows, g, s_idx > t_idx, s_idx <= t_idx)
+
+        @pl.when(me > 0)
+        def _():
+            p_copy(g).wait_recv()
+
+        @pl.when(g + AHEAD < groups)
+        def _():
+            send_product(g + AHEAD)
+
+        gain = skip_ref[pl.ds(g, 1), :]
+        own_p = [prod[g, b] for b in range(batch)]
+        ext_p = jnp.concatenate(
+            [jnp.concatenate([prod_halo[g, b] for b in range(batch)], 1), jnp.concatenate(own_p, 1)], 0
+        )
+        forward = banded(fwd_band, ext_p)
+        for b in range(batch):
+            at = slice(b * LANES, (b + 1) * LANES)
+            mixer = forward[:, at] + gain * own_p[b].astype(jnp.float32)
+            mixed_ref[b, :, cols] = (q_ref[b, :, cols].astype(jnp.float32) * mixer).astype(jnp.bfloat16)
+            gq_ref[b, :, cols] = (go_ref[b, :, cols].astype(jnp.float32) * mixer).astype(jnp.bfloat16)
+
     @pl.loop(0, groups)
     def _(g):
         cols = lanes_of(g)
-        build_bands(g)
-
-        @pl.when(me > 0)
-        def _():
-            p_copy(g).wait_recv()
+        build_band(bwd_band, bwd_rows, g, s_idx >= t_idx, s_idx < t_idx)
 
         @pl.when(me < n - 1)
         def _():
             g_copy(g).wait_recv()
 
-        @pl.when(g + in_flight < groups)
-        def _():
-            start_halo(g + in_flight)
+        @pl.when(g >= groups - AHEAD)
+        def _():
+            send_product(g + AHEAD - groups)
 
         gain = skip_ref[pl.ds(g, 1), :]
         own_p = [prod[g, b] for b in range(batch)]
         own_g = [gmix[g, b] for b in range(batch)]
-        ext_p = jnp.concatenate(
-            [jnp.concatenate([prod_halo[g, b] for b in range(batch)], 1), jnp.concatenate(own_p, 1)], 0
-        )
         ext_g = jnp.concatenate(
             [jnp.concatenate(own_g, 1), jnp.concatenate([gmix_halo[g, b] for b in range(batch)], 1)], 0
         )
-        forward = banded(fwd_band, ext_p)
         backward = banded(bwd_band, ext_g)
         skip_sum = jnp.zeros((1, LANES), jnp.float32)
         for b in range(batch):
             pf = own_p[b].astype(jnp.float32)
             gf = own_g[b].astype(jnp.float32)
             at = slice(b * LANES, (b + 1) * LANES)
-            mixer = forward[:, at] + gain * pf
             grad_p = backward[:, at] + gain * gf
-            mixed_ref[b, :, cols] = (q_ref[b, :, cols].astype(jnp.float32) * mixer).astype(jnp.bfloat16)
-            gq_ref[b, :, cols] = (go_ref[b, :, cols].astype(jnp.float32) * mixer).astype(jnp.bfloat16)
             gk_ref[b, :, cols] = (v_ref[b, :, cols].astype(jnp.float32) * grad_p).astype(jnp.bfloat16)
             gv_ref[b, :, cols] = (k_ref[b, :, cols].astype(jnp.float32) * grad_p).astype(jnp.bfloat16)
             skip_sum = skip_sum + jnp.sum(pf * gf, axis=0, keepdims=True)
@@ -262,6 +291,8 @@
     def wait_bytes(buffer, count, sem):
         pltpu.make_async_copy(buffer.at[pl.ds(0, count)], buffer.at[pl.ds(0, count)], sem).wait()
 
+    pl.loop(0, groups // 4)(forward_step)
+
     @pl.when(me < groups)
     def _():
         wait_bytes(terms, n - 1, rs_recv)
@@ -281,6 +312,10 @@
                 device_id_type=MESH,
             ).start()
 
+    pl.loop(groups // 4, groups // 2)(forward_step)
+
+    @pl.when(me < groups)
+    def _():
         wait_bytes(reduced, groups - 1, ag_recv)
 
     @pl.when(me >= groups)
@@ -300,7 +335,9 @@
         device_id_type=MESH,
     )
     swap.start()
-    fil_t = fil.T
+    pl.loop(groups // 2, groups * 3 // 4)(forward_step)
+    fil_t = reduced[:, :per_group, :].reshape(groups * per_group, taps).T
+    skp = reduced[:, per_group, :]
     swap.wait()
     both = squares[0] + squares[1]
     fil_mean = jnp.sum(both[0:8]) / fil_entries
@@ -308,6 +345,8 @@
     fu_ref[...] = fil_t / jnp.sqrt(jnp.full(fil_t.shape, fil_mean, jnp.float32) + 1e-06)
     su_ref[...] = skp / jnp.sqrt(jnp.full(skp.shape, skip_mean, jnp.float32) + 1e-06)
 
+    pl.loop(groups * 3 // 4, groups)(forward_step)
+
     @pl.loop(0, groups)
     def _(g):
         @pl.when(me < n - 1)
@@ -328,7 +367,7 @@
         wait_bytes(part, groups, rs_send)
 
 
-def on_device(in_flight, queries, key_input, value_input, filters, skip_gain, grad_output):
+def on_device(queries, key_input, value_input, filters, skip_gain, grad_output):
     batch, rows, channels = queries.shape
     taps, filter_count = filters.shape
     groups = channels // LANES
@@ -337,10 +376,11 @@
     cores = lax.axis_size("tp")
     entries = (float(taps * filter_count * cores), float(channels * cores))
     vmem = pl.BlockSpec(memory_space=pltpu.VMEM)
+    hbm = pl.BlockSpec(memory_space=pltpu.HBM)
     chunk = (groups, batch, rows, LANES)
     act = jax.ShapeDtypeStruct(queries.shape, jnp.bfloat16)
     outs = pl.pallas_call(
-        functools.partial(step_kernel, n, groups, in_flight, entries),
+        functools.partial(step_kernel, n, groups, entries),
         out_shape=(
             act,
             act,
@@ -349,9 +389,10 @@
             jax.ShapeDtypeStruct((taps, filter_count), jnp.float32),
             jax.ShapeDtypeStruct((groups, LANES), jnp.float32),
         ),
-        in_specs=[vmem] * 6,
+        in_specs=[vmem] * 2 + [hbm] * 4,
         out_specs=(vmem,) * 6,
-        scratch_shapes=[
+        scratch_shapes=[pltpu.VMEM(queries.shape, jnp.bfloat16)] * 4
+        + [
             pltpu.VMEM(chunk, jnp.bfloat16),
             pltpu.VMEM(chunk, jnp.bfloat16),
             pltpu.VMEM(chunk, jnp.bfloat16),
@@ -364,6 +405,7 @@
             pltpu.VMEM((n, 16, LANES), jnp.float32),
             pltpu.VMEM((groups, 16, LANES), jnp.float32),
             pltpu.VMEM((2, 16, LANES), jnp.float32),
+            pltpu.SemaphoreType.DMA((4, LOADS)),
             pltpu.SemaphoreType.DMA((groups,)),
             pltpu.SemaphoreType.DMA((groups,)),
             pltpu.SemaphoreType.DMA((groups,)),
@@ -376,7 +418,7 @@
             pltpu.SemaphoreType.DMA,
         ],
         compiler_params=pltpu.CompilerParams(
-            collective_id=0, has_side_effects=True, vmem_limit_bytes=48 * 1024 * 1024
+            collective_id=0, has_side_effects=True, vmem_limit_bytes=49 * 1024 * 1024
         ),
     )(filters, skip_gain.reshape(groups, LANES), queries, key_input, value_input, grad_output)
     return (*outs[:5], outs[5].reshape(channels))
@@ -385,7 +427,7 @@
 def solution(mesh):
     act = P(None, "ctx", "tp")
     return jax.shard_map(
-        functools.partial(on_device, 16),
+        on_device,
         mesh=mesh,
         in_specs=(act, act, act, P(None, "tp"), P("tp"), act),
         out_specs=(act, act, act, act, P(None, "tp"), P("tp")),

time: 76.3 us -> 63.7 us (0.83)
  Pallas kernels: 67.6 us -> 56.1 us
  local copies, waits for them, and re-layouts: 7.78 us -> 6.56 us
    pallas_call x1, Pallas kernels: 67.6 us -> 56.1 us  [on_device(): pl.pallas_call(functools.partial(step_kernel, n, groups, entries), out_sh...]
    unnamed x12 -> x10, local copies, waits for them, and re-layouts: 7.78 us -> 6.56 us
where the time goes in v2:
time: 63.7 us; the launch traced here: 63.3 us
  Pallas kernels  56.1 us (88%)
  local copies, waits for them, and re-layouts  6.56 us (10%)
  between operations  0.65 us (1%)
    pallas_call x1, Pallas kernels, on_device(): pl.pallas_call(functools.partial(step_kernel, n, groups, entries), out_sh...  56.1 us
    unnamed x10, local copies, waits for them, and re-layouts  6.56 us

profile of v2, /device:TPU:0, one launch (start us, length us, event | category | flops | bytes accessed | tf_op | source)
XLA Modules:
  0.0 63.3 jit_solution(12636459177999405274)
XLA Ops:
  0.6 0.0 copy-start
  0.6 0.7 %copy-done = bf16[128,128]{1,0:T(8,128)(2,1)S(1)} copy-done((bf16[128,128]{1,0:T(8,128)(2,1)S(1)}, bf16[128,128]{1,0:T(8,128)(2,1)}, u32[]{:S(2)}) %copy-start) | copy-done | bytes 32792
  1.4 0.0 copy-start.1
  1.4 0.7 %copy-done.1 = f32[2048]{0:T(1024)S(1)} copy-done((f32[2048]{0:T(1024)S(1)}, f32[2048]{0:T(1024)}, u32[]{:S(2)}) %copy-start.1) | copy-done | bytes 8216
  2.1 56.1 %shard_map.109 = (bf16[2,128,2048]{2,1,0:T(8,128)(2,1)S(1)}, bf16[2,128,2048]{2,1,0:T(8,128)(2,1)S(1)}, bf16[2,128,2048]{2,1,0:T(8,128)(2,1)S(1)}, bf16[2,128,20...) custom-call(bf16[128,128]{1,0:T(8,128)(2,1)S(1)} %copy-done, f32[16,128]{1,0:T(8,128)S(1)} %bitcast.2, ...), custom_call_target="tpu_custom_call" | custom-call | tf_op jit(solution)/shard_map/pallas_call | solution.py:382
  58.2 1.0 %copy.18 = bf16[2,128,2048]{2,1,0:T(8,128)(2,1)} copy(bf16[2,128,2048]{2,1,0:T(8,128)(2,1)S(1)} %get-tuple-element.24) | data formatting | bytes 2097152
  59.1 1.0 %copy.19 = bf16[2,128,2048]{2,1,0:T(8,128)(2,1)} copy(bf16[2,128,2048]{2,1,0:T(8,128)(2,1)S(1)} %get-tuple-element.25) | data formatting | bytes 2097152
  60.1 1.0 %copy.20 = bf16[2,128,2048]{2,1,0:T(8,128)(2,1)} copy(bf16[2,128,2048]{2,1,0:T(8,128)(2,1)S(1)} %get-tuple-element.26) | data formatting | bytes 2097152
  61.1 1.0 %copy.21 = bf16[2,128,2048]{2,1,0:T(8,128)(2,1)} copy(bf16[2,128,2048]{2,1,0:T(8,128)(2,1)S(1)} %get-tuple-element.27) | data formatting | bytes 2097152
  62.0 0.6 copy.22
  62.7 0.6 copy.23
Async XLA Ops:
  0.6 0.8 %copy-start = (bf16[128,128]{1,0:T(8,128)(2,1)S(1)}, bf16[128,128]{1,0:T(8,128)(2,1)}, u32[]{:S(2)}) copy-start(bf16[128,128]{1,0:T(8,128)(2,1)} %filt_ref.1) | copy-start | bytes 98308
  1.4 0.7 %copy-start.1 = (f32[2048]{0:T(1024)S(1)}, f32[2048]{0:T(1024)}, u32[]{:S(2)}) copy-start(f32[2048]{0:T(1024)} %param.10) | copy-start | bytes 24580
